TPU v7x, 256 devices: a whole 4x4x8 slice. The times are simulated.
256 devices in a mesh: expert: 32 (over y, x, core), tensor: 8 (over z).
Axes of the slice: x: 4, y: 4, z: 8, core: 2. Of those that a mesh axis runs over, the one named last changes fastest.
Arguments:
- tokens: bfloat16 [16384, 4096], P('expert', 'tensor'), may hold values from -36 to 36
- expert_ids: int32 [16384, 1], P('expert'), may hold values from 0 to 63; in each aligned block of 512 rows (0 to 511, 512 to 1023, ...) at most 16 rows name the same one
- gates: float32 [16384, 1], P('expert'), may hold values from 0.25 to 1
- expert_in: bfloat16 [64, 4096, 2048], P('expert', 'tensor'), may hold values from -0.09375 to 0.09375
- expert_out: bfloat16 [64, 2048, 4096], P('expert', None, 'tensor'), may hold values from -0.125 to 0.125
- norm_gain: float32 [4096], replicated, may hold values from 0.5 to 2
- up_weight: bfloat16 [4096, 8192], P('expert', 'tensor'), may hold values from -0.09375 to 0.09375
- down_weight: bfloat16 [4096, 8192], P('expert', 'tensor'), may hold values from -0.0625 to 0.0625
Outputs:
- layer_output: bfloat16 [16384, 4096], P('expert', 'tensor')
Inputs may be any that keep to these rules, and one draw needn't show every extreme that they name: `expert_ids`: among the 512 tokens of one block, at most 16 carry the same expert id; in some blocks one id is carried by exactly 16 tokens.
All inputs are finite; a program needn't handle non-finite values.
Results may differ from a plain program's by a relative error of at most 0.015.
Values may be sent and summed in bfloat16 or wider, within the bound.
No kernel may reach another device: no remote copies, remote signals or barrier semaphores. Data moves between devices by JAX's collectives and lax.ppermute only.
A program may use at most 128 MiB of HBM per device.

v0:
```python
import jax
import jax.numpy as jnp
from jax import lax
from jax.sharding import PartitionSpec as P

EXP_DEV = 2


def slot_table(expert_col, experts, capacity):
    expert = expert_col[:, 0]
    onehot = (expert[:, None] == jnp.arange(experts, dtype=jnp.int32)[None, :]).astype(jnp.int32)
    before = jnp.cumsum(onehot, axis=0) - onehot
    position = jnp.sum(before * onehot, axis=1)
    slot_index = expert * capacity + position
    selector = jnp.arange(experts * capacity, dtype=jnp.int32)[:, None] == slot_index[None, :]
    return selector.astype(jnp.bfloat16)


def trade(buffer):
    result = lax.all_to_all(buffer, "expert", split_axis=0, concat_axis=0, tiled=True)
    return result


def gather_rows(weight, combine, start_value):
    return combine(start_value, lax.all_gather(weight, "expert", axis=0, tiled=True), jnp.int32(0))


def shards(tokens, expert_ids, gates, expert_in, expert_out, norm_gain, up_weight, down_weight):
    token_count = tokens.shape[0]
    local_width = tokens.shape[1]
    groups = lax.axis_size("expert")
    experts = EXP_DEV * groups
    capacity = 2 * token_count // experts
    selector = slot_table(expert_ids, experts, capacity)
    outgoing = jnp.dot(selector, tokens, preferred_element_type=jnp.float32).astype(jnp.bfloat16)
    outgoing = outgoing.reshape(groups, EXP_DEV, capacity, local_width)
    arrived = trade(outgoing)
    partial_value = jnp.einsum(
        "sjcd,jdh->sjch", arrived, expert_in, preferred_element_type=jnp.float32
    )
    summed = lax.psum(partial_value.astype(jnp.bfloat16), "tensor").astype(jnp.float32)
    active = jax.nn.relu(summed).astype(jnp.bfloat16)
    produced = jnp.einsum(
        "sjch,jhd->sjcd", active, expert_out, preferred_element_type=jnp.float32
    ).astype(jnp.bfloat16)
    returned = trade(produced).reshape(experts * capacity, local_width)
    routed = lax.dot_general(
        selector, returned, (((0,), (0,)), ((), ())), preferred_element_type=jnp.float32
    )
    mixed = (tokens.astype(jnp.float32) + gates * routed).astype(jnp.bfloat16)
    whole = lax.all_gather(mixed, "tensor", axis=1, tiled=True)
    whole_f32 = whole.astype(jnp.float32)
    mean_square = jnp.mean(whole_f32 * whole_f32, axis=1, keepdims=True)
    normed = (whole_f32 * lax.rsqrt(mean_square + 1e-06) * norm_gain).astype(jnp.bfloat16)

    def add_up(carry, piece, start):
        return jnp.dot(normed, piece, preferred_element_type=jnp.float32)

    ffn_hidden = gather_rows(
        up_weight, add_up, jnp.zeros((token_count, up_weight.shape[1]), jnp.float32)
    )
    ffn_active = jax.nn.gelu(ffn_hidden, approximate=True).astype(jnp.bfloat16)

    def add_down(carry, piece, start):
        contribution = lax.dot_general(
            ffn_active, piece, (((1,), (1,)), ((), ())), preferred_element_type=jnp.float32
        )
        return contribution

    outputs = gather_rows(
        down_weight, add_down, jnp.zeros((token_count, whole.shape[1]), jnp.float32)
    )
    summed_out = lax.psum_scatter(
        outputs.astype(jnp.bfloat16), "tensor", scatter_dimension=1, tiled=True
    ).astype(jnp.float32)
    return (mixed.astype(jnp.float32) + summed_out).astype(jnp.bfloat16)


def solution(mesh):
    return jax.shard_map(
        shards,
        mesh=mesh,
        in_specs=(
            P("expert", "tensor"),
            P("expert", None),
            P("expert", None),
            P("expert", "tensor", None),
            P("expert", None, "tensor"),
            P(),
            P("expert", "tensor"),
            P("expert", "tensor"),
        ),
        out_specs=P("expert", "tensor"),
        check_vma=False,
    )
```

profile of v0, /device:TPU:1, one launch (start us, length us, event | category | flops | bytes accessed | tf_op | source)
XLA Modules:
  0.0 424.8 jit_solution(10991581283528540992)
XLA Ops:
  6.5 0.7 fusion.42
  7.2 1.2 reduce-window.6
  8.4 0.2 slice_reduce_fusion
  8.7 0.9 fusion.41
  9.7 0.9 multiply_add_fusion
  10.6 1.8 fusion.24
  12.4 25.6 %all_to_all.10 = bf16[32,2,16,512]{3,2,1,0:T(8,128)(2,1)S(1)} all-to-all(bf16[32,2,16,512]{3,2,1,0:T(8,128)(2,1)S(1)} %bitcast.50), channel_id=1, replica_groups=mesh['expert'=32,'tensor'=8] {'expert'}, dimensions={0} | all-to-all | bytes 2097152 | tf_op jit(solution)/shard_map/all_to_all | solution.py:20
  37.9 4.3 %convert_bitcast_fusion = bf16[32,2,16,2048]{3,2,0,1:T(8,128)(2,1)} fusion(bf16[2,512,2048]{2,1,0:T(8,128)(2,1)S(1)} %copy-done.1, bf16[32,2,16,512]{3,2,1,0:T(8,128)(2,1)S(1)} %all_to_all.10), kind=kOutput, calls=%fused_computation.15 | convolution fusion | flops 2149580800 | bytes 9437184 | tf_op jit(solution)/shard_map/sjcd,jdh->sjch/dot_general | solution.py:38
  42.3 108.1 %all-reduce.2.cloned.1.call-done = bf16[32,2,16,2048]{3,2,0,1:T(8,128)(2,1)} async-done(((bf16[32,2,16,2048]{3,2,0,1:T(8,128)(2,1)}), bf16[32,2,16,2048]{3,2,0,1:T(8,128)(2,1)}) %all-reduce.2.cloned.1.call-update) | async-done | bytes 4194320 | tf_op jit(solution)/shard_map/psum | solution.py:41
  150.4 5.8 %fusion.30 = bf16[32,2,16,512]{3,2,0,1:T(8,128)(2,1)S(1)} fusion(bf16[2,2048,512]{2,1,0:T(8,128)(2,1)} %param.12, bf16[32,2,16,2048]{3,2,0,1:T(8,128)(2,1)} %all-reduce.2.cloned.1.call-done), kind=kOutput, calls=%fused_computation.30 | convolution fusion | flops 2154299392 | bytes 9437184 | tf_op jit(solution)/shard_map/sjch,jhd->sjcd/dot_general | solution.py:43
  156.2 0.1 copy.16
  156.3 24.6 %all_to_all.11 = bf16[32,2,16,512]{3,2,1,0:T(8,128)(2,1)S(1)} all-to-all(bf16[32,2,16,512]{3,2,1,0:T(8,128)(2,1)S(1)} %copy.16), channel_id=1, replica_groups=mesh['expert'=32,'tensor'=8] {'expert'}, dimensions={0} | all-to-all | bytes 2097152 | tf_op jit(solution)/shard_map/all_to_all | solution.py:20
  180.9 1.6 fusion.35
  182.6 0.7 all-gather.6.cloned.1.call-update
  183.3 0.5 all-gather.8.cloned.1.call-update
  183.8 0.2 reduce-scatter.2.cloned.1.call-start
  184.1 48.4 %all-gather.4.cloned.1.call-done = bf16[512,4096]{1,0:T(8,128)(2,1)} async-done(((bf16[512,512]{1,0:T(8,128)(2,1)}), bf16[512,4096]{1,0:T(8,128)(2,1)}) %all-gather.4.cloned.1.call-update) | async-done | bytes 4194320 | tf_op jit(solution)/shard_map/all_gather | solution.py:51
  232.4 3.1 fusion
  235.5 56.4 %all-gather.6.cloned.1.call-done = bf16[4096,1024]{1,0:T(8,128)(2,1)} async-done(((bf16[128,1024]{1,0:T(8,128)(2,1)}), bf16[4096,1024]{1,0:T(8,128)(2,1)}) %all-gather.6.cloned.1.call-update) | async-done | bytes 8388624 | tf_op jit(solution)/shard_map/all_gather | solution.py:25
  292.0 9.6 %fusion.21 = bf16[512,1024]{1,0:T(8,128)(2,1)S(1)} fusion(bf16[4096,1024]{1,0:T(8,128)(2,1)} %all-gather.6.cloned.1.call-done, bf16[512,4096]{1,0:T(8,128)(2,1)} %all-gather.4.cloned.1.call-done, f32[4096]{0:T(1024)S(1)} %copy-done.3, f32[512]{0:T(512)S(1)} %add_rsqrt_fusion), kind=kOutput, calls=%fused_computation.24 | convolution fusion | flops 4308074496 | bytes 13649920 | tf_op jit(solution)/shard_map/dot_general | solution.py:57
  301.6 50.4 %all-gather.8.cloned.1.call-done = bf16[4096,1024]{1,0:T(8,128)(2,1)} async-done(((bf16[128,1024]{1,0:T(8,128)(2,1)}), bf16[4096,1024]{1,0:T(8,128)(2,1)}) %all-gather.8.cloned.1.call-update) | async-done | bytes 8388624 | tf_op jit(solution)/shard_map/all_gather | solution.py:25
  352.0 9.5 %convolution_convert_fusion = bf16[512,4096]{1,0:T(8,128)(2,1)} fusion(bf16[512,1024]{1,0:T(8,128)(2,1)S(1)} %fusion.21, bf16[4096,1024]{1,0:T(8,128)(2,1)} %all-gather.8.cloned.1.call-done), kind=kOutput, calls=%fused_computation.6 | convolution fusion | flops 4297064448 | bytes 13631488 | tf_op jit(solution)/shard_map/dot_general | solution.py:65
  361.5 54.7 %reduce-scatter.2.cloned.1.call-done = bf16[512,512]{1,0:T(8,128)(2,1)} async-done(((bf16[512,4096]{1,0:T(8,128)(2,1)}), bf16[512,512]{1,0:T(8,128)(2,1)}) %reduce-scatter.2.cloned.1.call-update) | async-done | bytes 524304 | tf_op jit(solution)/shard_map/reduce_scatter | solution.py:73
  416.3 2.0 add_convert_fusion
  (20 shorter events, 0.2 us)
Async XLA Ops:
  6.5 143.8 %all-reduce.2.cloned.1.call-start = ((), (), s32[]{:S(2)}) async-start(), calls=%async_computation.3 | async-start | bytes 8388608 | tf_op jit(solution)/shard_map/psum | solution.py:41
  8.7 29.2 %copy-start.1 = (bf16[2,512,2048]{2,1,0:T(8,128)(2,1)S(1)}, bf16[2,512,2048]{2,1,0:T(8,128)(2,1)}, u32[]{:S(2)}) copy-start(bf16[2,512,2048]{2,1,0:T(8,128)(2,1)} %param.11) | copy-start | bytes 12582916
  42.3 190.2 %all-gather.4.cloned.1.call-start = ((), (), s32[]{:S(2)}) async-start(), calls=%async_computation.4 | async-start | bytes 4718592 | tf_op jit(solution)/shard_map/all_gather | solution.py:51
  156.2 24.7 %copy-start.2 = (bf16[512,512]{1,0:T(8,128)(2,1)S(1)}, bf16[512,512]{1,0:T(8,128)(2,1)}, u32[]{:S(2)}) copy-start(bf16[512,512]{1,0:T(8,128)(2,1)} %param.8) | copy-start | bytes 1572868
  156.2 24.7 %copy-start.4 = (f32[512,1]{0,1:T(1,128)S(1)}, f32[512,1]{0,1:T(1,128)}, u32[]{:S(2)}) copy-start(f32[512,1]{0,1:T(1,128)} %param.10) | copy-start | bytes 6148
  180.9 111.0 %copy-start.3 = (f32[4096]{0:T(1024)S(1)}, f32[4096]{0:T(1024)}, u32[]{:S(2)}) copy-start(f32[4096]{0:T(1024)} %param.13) | copy-start | bytes 49156
  182.5 109.4 %all-gather.6.cloned.1.call-start = ((), (), s32[]{:S(2)}) async-start(), calls=%async_computation.5 | async-start | bytes 8650752 | tf_op jit(solution)/shard_map/all_gather | solution.py:25
  183.3 168.7 %all-gather.8.cloned.1.call-start = ((), (), s32[]{:S(2)}) async-start(), calls=%async_computation.6 | async-start | bytes 8650752 | tf_op jit(solution)/shard_map/all_gather | solution.py:25
  183.8 232.4 %reduce-scatter.2.cloned.1.call-start = ((), (), s32[]{:S(2)}) async-start(), calls=%async_computation.7 | async-start | bytes 4718592 | tf_op jit(solution)/shard_map/reduce_scatter | solution.py:73
  361.5 54.8 %copy-start = (bf16[512,512]{1,0:T(8,128)(2,1)S(1)}, bf16[512,512]{1,0:T(8,128)(2,1)}, u32[]{:S(2)}) copy-start(bf16[512,512]{1,0:T(8,128)(2,1)} %fusion.35) | copy-start | bytes 1572868
Sparse Core Ops, SparseCore 0:
  42.4 107.9 all-reduce.1
  182.6 49.7 all-gather.3
  235.0 56.9 all-gather.5
  294.4 57.5 all-gather.7
  361.6 54.5 reduce-scatter.1
where the time goes:
time: 425 us
  waiting for transfers between devices  319 us (75%)
  blocking collectives  50.2 us (12%)
  matrix products  32.6 us (8%)
  between operations  13.2 us (3%)
  other arithmetic  8.86 us (2%)
    psum x1, waiting for transfers between devices, shards(): lax.psum(partial_value.astype(jnp.bfloat16), 'tensor').astype(jnp.float32)  108 us
    all_gather x2, waiting for transfers between devices, gather_rows(): lax.all_gather(weight, 'expert', axis=0, tiled=True)  107 us
    reduce_scatter x1, waiting for transfers between devices, shards(): lax.psum_scatter(outputs.astype(jnp.bfloat16), 'tensor', scatter_dimensio...  54.7 us
    all_to_all x2, blocking collectives, trade(): lax.all_to_all(buffer, 'expert', split_axis=0, concat_axis=0, tiled=True)  50.2 us
    all_gather x1, waiting for transfers between devices, shards(): whole = lax.all_gather(mixed, 'tensor', axis=1, tiled=True)  48.4 us
    dot_general x1, matrix products, add_up(): return jnp.dot(normed, piece, preferred_element_type=jnp.float32)  9.58 us
    dot_general x1, matrix products, add_down(): lax.dot_general(ffn_active, piece, (((1,), (1,)), ((), ())), preferred_el...  9.54 us
  transfers between devices with their start and end apart: 5, of which 5 were waited for; matrix products, arithmetic and copies ran while one was open for 3% of the time, Pallas kernels for 0%

commit v1 on v0

--- a/solution.py
+++ b/solution.py
@@ -1,9 +1,18 @@
+import functools
 import jax
 import jax.numpy as jnp
 from jax import lax
 from jax.sharding import PartitionSpec as P
 
 EXP_DEV = 2
+
+
+def return_all_views(x_local, comm_axis):
+    opened = jnp.sum(lax.all_gather(x_local, comm_axis), axis=0)
+    return opened
+
+
+_try_all_circles = functools.partial(return_all_views, comm_axis="tensor")
 
 
 def slot_table(expert_col, experts, capacity):
@@ -38,7 +47,7 @@
     partial_value = jnp.einsum(
         "sjcd,jdh->sjch", arrived, expert_in, preferred_element_type=jnp.float32
     )
-    summed = lax.psum(partial_value.astype(jnp.bfloat16), "tensor").astype(jnp.float32)
+    summed = _try_all_circles(partial_value.astype(jnp.bfloat16)).astype(jnp.float32)
     active = jax.nn.relu(summed).astype(jnp.bfloat16)
     produced = jnp.einsum(
         "sjch,jhd->sjcd", active, expert_out, preferred_element_type=jnp.float32

time: 425 us -> 660 us (1.55)
  waiting for transfers between devices: 319 us -> 540 us
  other arithmetic: 8.86 us -> 23.1 us
    all_gather x0 -> x1, waiting for transfers between devices: none -> 329 us  [return_all_views(): opened = jnp.sum(lax.all_gather(x_local, comm_axis), axis=0)]
    psum x1 -> x0, waiting for transfers between devices: 108 us -> none  [shards(): lax.psum(partial_value.astype(jnp.bfloat16), 'tensor').astype(jnp.float32)]
    reduce_sum x0 -> x1, other arithmetic: none -> 14.2 us  [return_all_views(): opened = jnp.sum(lax.all_gather(x_local, comm_axis), axis=0)]
  transfers between devices with their start and end apart: 5 -> 5, of which waited for: 5 -> 5; matrix products, arithmetic and copies ran while one was open for 3% -> 2% of each run, Pallas kernels for 0% -> 0%
where the time goes in v1:
time: 660 us
  waiting for transfers between devices  540 us (82%)
  blocking collectives  50.2 us (8%)
  matrix products  32.7 us (5%)
  other arithmetic  23.1 us (4%)
  between operations  13.2 us (2%)
    all_gather x1, waiting for transfers between devices, return_all_views(): opened = jnp.sum(lax.all_gather(x_local, comm_axis), axis=0)  329 us
    all_gather x2, waiting for transfers between devices, gather_rows(): lax.all_gather(weight, 'expert', axis=0, tiled=True)  107 us
    reduce_scatter x1, waiting for transfers between devices, shards(): lax.psum_scatter(outputs.astype(jnp.bfloat16), 'tensor', scatter_dimensio...  54.7 us
    all_to_all x2, blocking collectives, trade(): lax.all_to_all(buffer, 'expert', split_axis=0, concat_axis=0, tiled=True)  50.2 us
    all_gather x1, waiting for transfers between devices, shards(): whole = lax.all_gather(mixed, 'tensor', axis=1, tiled=True)  48.3 us
    reduce_sum x1, other arithmetic, return_all_views(): opened = jnp.sum(lax.all_gather(x_local, comm_axis), axis=0)  14.2 us
  transfers between devices with their start and end apart: 5, of which 5 were waited for; matrix products, arithmetic and copies ran while one was open for 2% of the time, Pallas kernels for 0%

profile of v1, /device:TPU:1, one launch (start us, length us, event | category | flops | bytes accessed | tf_op | source)
XLA Modules:
  0.0 660.1 jit_solution(4898327029020504856)
XLA Ops:
  6.5 0.7 fusion.42
  7.2 1.2 reduce-window.6
  8.4 0.2 slice_reduce_fusion
  8.7 0.9 fusion.41
  9.7 0.9 multiply_add_fusion
  10.6 1.8 fusion.24
  12.4 25.6 %all_to_all.10 = bf16[32,2,16,512]{3,2,1,0:T(8,128)(2,1)S(1)} all-to-all(bf16[32,2,16,512]{3,2,1,0:T(8,128)(2,1)S(1)} %bitcast.52), channel_id=1, replica_groups=mesh['expert'=32,'tensor'=8] {'expert'}, dimensions={0} | all-to-all | bytes 2097152 | tf_op jit(solution)/shard_map/all_to_all | solution.py:29
  37.9 4.4 convert_bitcast_fusion
  42.4 329.1 %all-gather.12.cloned.1.call-done = bf16[256,2,16,2048]{3,2,0,1:T(8,128)(2,1)} async-done(((bf16[32,2,16,2048]{3,2,0,1:T(8,128)(2,1)}), bf16[256,2,16,2048]{3,2,0,1:T(8,128)(2,1)}) %all-gather.12.cloned.1.call-update) | async-done | bytes 33554448 | tf_op jit(solution)/shard_map/all_gather | solution.py:11
  371.5 14.2 %reduce_sum.31 = bf16[32,2,16,2048]{3,2,0,1:T(8,128)(2,1)} reduce(bf16[8,32,2,16,2048]{4,3,1,0,2:T(8,128)(2,1)} %bitcast.50, bf16[]{:T(256)} %constant.7.clone.1), dimensions={0}, to_apply=%region_3.4 | reduce | flops 14680064 | bytes 37748736 | tf_op jit(solution)/shard_map/reduce_sum | solution.py:11
  385.8 5.8 fusion.30
  391.7 24.6 %all_to_all.11 = bf16[32,2,16,512]{3,2,1,0:T(8,128)(2,1)S(1)} all-to-all(bf16[32,2,16,512]{3,2,1,0:T(8,128)(2,1)S(1)} %copy.15), channel_id=1, replica_groups=mesh['expert'=32,'tensor'=8] {'expert'}, dimensions={0} | all-to-all | bytes 2097152 | tf_op jit(solution)/shard_map/all_to_all | solution.py:29
  416.3 1.6 fusion.35
  417.9 0.7 all-gather.8.cloned.1.call-update
  418.7 0.5 all-gather.10.cloned.1.call-update
  419.2 0.2 reduce-scatter.2.cloned.1.call-start
  419.4 48.3 %all-gather.6.cloned.1.call-done = bf16[512,4096]{1,0:T(8,128)(2,1)} async-done(((bf16[512,512]{1,0:T(8,128)(2,1)}), bf16[512,4096]{1,0:T(8,128)(2,1)}) %all-gather.6.cloned.1.call-update) | async-done | bytes 4194320 | tf_op jit(solution)/shard_map/all_gather | solution.py:60
  467.7 3.1 fusion
  470.8 56.4 %all-gather.8.cloned.1.call-done = bf16[4096,1024]{1,0:T(8,128)(2,1)} async-done(((bf16[128,1024]{1,0:T(8,128)(2,1)}), bf16[4096,1024]{1,0:T(8,128)(2,1)}) %all-gather.8.cloned.1.call-update) | async-done | bytes 8388624 | tf_op jit(solution)/shard_map/all_gather | solution.py:34
  527.3 9.6 %fusion.21 = bf16[512,1024]{1,0:T(8,128)(2,1)S(1)} fusion(bf16[4096,1024]{1,0:T(8,128)(2,1)} %all-gather.8.cloned.1.call-done, bf16[512,4096]{1,0:T(8,128)(2,1)} %all-gather.6.cloned.1.call-done, f32[4096]{0:T(1024)S(1)} %copy-done.3, f32[512]{0:T(512)S(1)} %add_rsqrt_fusion), kind=kOutput, calls=%fused_computation.24 | convolution fusion | flops 4308074496 | bytes 13649920 | tf_op jit(solution)/shard_map/dot_general | solution.py:66
  536.9 50.4 %all-gather.10.cloned.1.call-done = bf16[4096,1024]{1,0:T(8,128)(2,1)} async-done(((bf16[128,1024]{1,0:T(8,128)(2,1)}), bf16[4096,1024]{1,0:T(8,128)(2,1)}) %all-gather.10.cloned.1.call-update) | async-done | bytes 8388624 | tf_op jit(solution)/shard_map/all_gather | solution.py:34
  587.3 9.5 %convolution_convert_fusion = bf16[512,4096]{1,0:T(8,128)(2,1)} fusion(bf16[512,1024]{1,0:T(8,128)(2,1)S(1)} %fusion.21, bf16[4096,1024]{1,0:T(8,128)(2,1)} %all-gather.10.cloned.1.call-done), kind=kOutput, calls=%fused_computation.6 | convolution fusion | flops 4297064448 | bytes 13631488 | tf_op jit(solution)/shard_map/dot_general | solution.py:74
  596.9 54.7 %reduce-scatter.2.cloned.1.call-done = bf16[512,512]{1,0:T(8,128)(2,1)} async-done(((bf16[512,4096]{1,0:T(8,128)(2,1)}), bf16[512,512]{1,0:T(8,128)(2,1)}) %reduce-scatter.2.cloned.1.call-update) | async-done | bytes 524304 | tf_op jit(solution)/shard_map/reduce_scatter | solution.py:82
  651.6 2.0 add_convert_fusion
  (21 shorter events, 0.3 us)
Async XLA Ops:
  6.5 365.0 %all-gather.12.cloned.1.call-start = ((), (), s32[]{:S(2)}) async-start(), calls=%async_computation.7 | async-start | bytes 37748736 | tf_op jit(solution)/shard_map/all_gather | solution.py:11
  8.7 29.2 %copy-start.1 = (bf16[2,512,2048]{2,1,0:T(8,128)(2,1)S(1)}, bf16[2,512,2048]{2,1,0:T(8,128)(2,1)}, u32[]{:S(2)}) copy-start(bf16[2,512,2048]{2,1,0:T(8,128)(2,1)} %param.11) | copy-start | bytes 12582916
  42.3 425.4 %all-gather.6.cloned.1.call-start = ((), (), s32[]{:S(2)}) async-start(), calls=%async_computation.3 | async-start | bytes 4718592 | tf_op jit(solution)/shard_map/all_gather | solution.py:60
  391.6 24.7 %copy-start.2 = (bf16[512,512]{1,0:T(8,128)(2,1)S(1)}, bf16[512,512]{1,0:T(8,128)(2,1)}, u32[]{:S(2)}) copy-start(bf16[512,512]{1,0:T(8,128)(2,1)} %param.8) | copy-start | bytes 1572868
  391.6 24.7 %copy-start.4 = (f32[512,1]{0,1:T(1,128)S(1)}, f32[512,1]{0,1:T(1,128)}, u32[]{:S(2)}) copy-start(f32[512,1]{0,1:T(1,128)} %param.10) | copy-start | bytes 6148
  416.3 111.0 %copy-start.3 = (f32[4096]{0:T(1024)S(1)}, f32[4096]{0:T(1024)}, u32[]{:S(2)}) copy-start(f32[4096]{0:T(1024)} %param.13) | copy-start | bytes 49156
  417.9 109.4 %all-gather.8.cloned.1.call-start = ((), (), s32[]{:S(2)}) async-start(), calls=%async_computation.4 | async-start | bytes 8650752 | tf_op jit(solution)/shard_map/all_gather | solution.py:34
  418.6 168.7 %all-gather.10.cloned.1.call-start = ((), (), s32[]{:S(2)}) async-start(), calls=%async_computation.5 | async-start | bytes 8650752 | tf_op jit(solution)/shard_map/all_gather | solution.py:34
  419.2 232.4 %reduce-scatter.2.cloned.1.call-start = ((), (), s32[]{:S(2)}) async-start(), calls=%async_computation.6 | async-start | bytes 4718592 | tf_op jit(solution)/shard_map/reduce_scatter | solution.py:82
  596.8 54.8 %copy-start = (bf16[512,512]{1,0:T(8,128)(2,1)S(1)}, bf16[512,512]{1,0:T(8,128)(2,1)}, u32[]{:S(2)}) copy-start(bf16[512,512]{1,0:T(8,128)(2,1)} %fusion.35) | copy-start | bytes 1572868
Sparse Core Ops, SparseCore 0:
  42.5 329.0 all-gather.11
  418.0 49.6 all-gather.5
  470.3 56.9 all-gather.7
  529.7 57.5 all-gather.9
  597.0 54.5 reduce-scatter.1
